TPU v7x, 512 devices: a whole 4x8x8 slice. The times are simulated.
512 devices in a mesh: wide: 64 (over z, y_lo, core), narrow: 8 (over y_hi, x).
Axes of the slice: x: 4, y: 8 (y_hi: 2, y_lo: 4; y = y_hi * 4 + y_lo), z: 8, core: 2. Of those that a mesh axis runs over, the one named last changes fastest.
Arguments:
- member_weights: bfloat16 [8, 128, 128, 128], P('narrow', 'wide'), may hold values from -6 to 6
- perturbations: bfloat16 [8, 3, 128, 128, 128], P('narrow', None, 'wide'), may hold values from -2 to 2
- vertical: bfloat16 [3, 128, 128], replicated, may hold values from -1 to 2
- obs_column: int32 [131072], P('wide'), may hold values from 0 to 255
- obs_level: int32 [131072], P('wide'), may hold values from 0 to 127
- obs_count: int32 [64], P('wide'), may hold values from 512 to 2048, as said below
- quality_flag: int32 [131072], P('wide'), may hold values 0 or 1
- obs_value: float32 [3, 131072], P(None, 'wide'), may hold values from -6 to 6
- obs_weight: float32 [3, 131072], P(None, 'wide'), may hold values from 1 to 10
Outputs:
- gradient: float32 [8, 128, 128, 128], P('narrow', 'wide')
Inputs may be any that keep to these rules, and one draw needn't show every extreme that they name: Each column block uses its first obs_count slots; at most 2048 observations a block, and some block holds exactly 2048.
All inputs are finite; a program needn't handle non-finite values. No bound on the sum of `quality_flag` on one device may be relied on, other than what follows from the above.
Results may differ from a plain program's by a relative error of at most 0.008.
Values may be sent and summed in bfloat16 or wider, within the bound.
A program may use at most 128 MiB of HBM per device.

v0:
```python
import jax
import jax.numpy as jnp
from jax import lax
from jax.sharding import PartitionSpec as P

scale_lengths = (1.5, 4.0, 12.0)
scale_mix = (0.6, 0.5, 0.4)


def gauss_table(length, spread):
    places = jnp.arange(length).astype(jnp.float32)
    offset = places[:, None] - places[None, :]
    norm_factor = jnp.sqrt(jnp.sqrt(jnp.float32(jnp.pi)) * spread)
    values = jnp.exp(-0.5 * offset * offset / (spread * spread)) / norm_factor
    values = jnp.where(jnp.abs(offset) <= 4.0 * spread, values, jnp.float32(0.0))
    return values.astype(jnp.bfloat16)


def local(
    member_weights,
    perturbations,
    vertical,
    obs_column,
    obs_level,
    obs_count,
    quality_flag,
    obs_value,
    obs_weight,
):
    width_x = member_weights.shape[2]
    width_y = member_weights.shape[3]
    tables = [
        (gauss_table(width_x, spread_len), gauss_table(width_y, spread_len))
        for spread_len in scale_lengths
    ]
    summed = None
    for (table_x, table_y), mix in zip(tables, scale_mix):
        across = jnp.einsum(
            "ix,mlxy->mliy", table_x, member_weights, preferred_element_type=jnp.float32
        ).astype(jnp.bfloat16)
        scaled = mix * jnp.einsum(
            "mliy,yz->milz", across, table_y, preferred_element_type=jnp.float32
        )
        summed = scaled if summed is None else summed + scaled
    localized = summed.astype(jnp.bfloat16)
    column_weights = lax.all_to_all(localized, "wide", split_axis=1, concat_axis=2, tiled=True)
    partial_total = jnp.einsum(
        "mvily,mily->vily", perturbations, column_weights, preferred_element_type=jnp.float32
    )
    slot_count = obs_column.shape[0]
    slots = jnp.arange(slot_count)
    live = (slots < obs_count[0]) & (quality_flag > 0)
    row_of = obs_column // width_y
    col_of = obs_column % width_y
    member_total = lax.psum(partial_total, "narrow")
    increment = jnp.einsum(
        "vlk,viky->vily",
        vertical,
        member_total.astype(jnp.bfloat16),
        preferred_element_type=jnp.float32,
    )
    share_width = increment.shape[3]
    local_col = col_of - 0
    inside = (local_col >= 0) & (local_col < share_width)
    safe_col = jnp.clip(local_col, 0, share_width - 1)
    at_obs = increment[:, row_of, obs_level, safe_col]
    misfit = jnp.where(
        (live & inside)[None, :], obs_weight * (at_obs - obs_value), jnp.float32(0.0)
    )
    spread_back = (
        jnp.zeros(increment.shape, jnp.float32).at[:, row_of, obs_level, safe_col].add(misfit)
    )
    obs_adjoint = spread_back.astype(jnp.bfloat16)
    vertical_adjoint = jnp.einsum(
        "vkl,viky->vily", vertical, obs_adjoint, preferred_element_type=jnp.float32
    ).astype(jnp.bfloat16)
    column_grad = jnp.einsum(
        "mvily,vily->mily", perturbations, vertical_adjoint, preferred_element_type=jnp.float32
    ).astype(jnp.bfloat16)
    level_grad = lax.all_to_all(column_grad, "wide", split_axis=2, concat_axis=1, tiled=True)
    gradient = member_weights.astype(jnp.float32)
    for (table_x, table_y), mix in zip(tables, scale_mix):
        back_rows = jnp.einsum(
            "mxlz,yz->mxly", level_grad, table_y, preferred_element_type=jnp.float32
        ).astype(jnp.bfloat16)
        gradient = gradient + mix * jnp.einsum(
            "ix,mily->mlxy", table_x, back_rows, preferred_element_type=jnp.float32
        )
    return gradient


def solution(mesh):
    placed = (
        P("narrow", "wide", None, None),
        P("narrow", None, "wide", None, None),
        P(),
        P("wide"),
        P("wide"),
        P("wide"),
        P("wide"),
        P(None, "wide"),
        P(None, "wide"),
    )
    return jax.shard_map(
        local,
        mesh=mesh,
        in_specs=placed,
        out_specs=P("narrow", "wide", None, None),
        check_vma=False,
    )
```

profile of v0, /device:TPU:1, one launch (start us, length us, event | category | flops | bytes accessed | tf_op | source)
XLA Modules:
  0.0 176.7 jit_solution(958969765738051365)
XLA Ops:
  0.0 0.0 copy-start
  0.0 1.2 convolution_multiply_fusion.5
  1.3 1.2 fusion.10
  2.5 1.2 fusion.18
  3.7 0.8 copy.52
  4.5 15.4 %all-to-all-start = ((bf16[1,128,2,128]{3,2,0,1:T(2,128)(2,1)}), bf16[1,128,2,128]{3,2,0,1:T(2,128)(2,1)S(1)}, u32[]{:S(2)}, u32[]{:S(2)}) async-start(bf16[1,128,2,128]{3,2,0,1:T(2,128)(2,1)} %copy.52), calls=%async_computation | async-start | bytes 131072 | tf_op jit(solution)/shard_map/all_to_all | solution.py:46
  19.9 0.7 compare_select_fusion.2
  20.6 0.7 compare_select_fusion.1
  21.4 0.7 multiply_reduce_fusion
  22.1 0.8 and_reduce_fusion
  22.9 1.1 copy.56
  24.0 1.1 copy.58
  25.1 1.1 copy.59
  26.9 1.1 copy.75
  28.0 0.7 fusion.105
  28.7 1.2 all-to-all-done
  30.0 0.1 copy.54
  30.1 0.1 copy.55
  30.3 48.8 %all-reduce.1 = bf16[3,2,128,128]{2,3,1,0:T(8,128)(2,1)S(1)} all-reduce(f32[3,2,128,128]{2,3,1,0:T(8,128)S(1)} %convert_multiply_fusion), channel_id=1, replica_groups=mesh['wide'=64,'narrow'=8] {'narrow'}, use_global_device_ids=true, to_apply=%region_0.1 | all-reduce | flops 98304 | bytes 589824 | tf_op jit(solution)/shard_map/psum | solution.py:55
  79.0 0.0 copy-done
  79.0 0.2 convolution_bitcast_fusion
  79.3 13.7 %copy.57 = f32[3,2,128,128]{0,3,2,1:T(8,128)} copy(f32[3,2,128,128]{2,3,1,0:T(8,128)S(1)} %convolution_bitcast_fusion) | data formatting | bytes 786432 | tf_op jit(solution)/shard_map/vlk,viky->vily/transpose | solution.py:56
  92.9 32.5 %scatter_custom_fusion = f32[3,32768]{0,1:T(8,128)} fusion(s32[2048]{0:T(1024)S(1)} %broadcast_select_fusion, f32[]{:T(128)} %constant.22.clone.1, f32[3,2048]{0,1:T(8,128)S(1)} %copy.59, f32[3,2048]{0,1:T(8,128)S(1)} %copy.58, pred[2048]{0:T(1024)(128)(4,1)S(1)} %fusion.105, f32[3,2,128,128]{0,3,2,1:T(8,128)} %copy.57, s32[2048]{0:T(1024)S(1)} %bitcast.160), kind=kCustom, calls=%fused_computation.2 | custom fusion | flops 24576 | bytes 19278848
  125.5 0.0 copy-start.1
  125.5 8.9 %convert_element_type.168 = bf16[3,32768]{0,1:T(8,128)(2,1)} convert(f32[3,32768]{0,1:T(8,128)} %scatter_custom_fusion) | non-fusion elementwise | flops 98304 | bytes 589824 | tf_op jit(solution)/shard_map/convert_element_type | solution.py:73
  134.4 11.1 %copy.60 = bf16[3,2,128,128]{2,3,1,0:T(8,128)(2,1)S(1)} copy(bf16[3,2,128,128]{0,3,2,1:T(8,128)(2,1)} %bitcast.143) | data formatting | bytes 393216 | tf_op jit(solution)/shard_map/convert_element_type | solution.py:73
  145.6 0.2 fusion.5
  145.8 0.8 copy.86
  146.5 18.0 %all-to-all-start.1 = ((bf16[1,2,128,128]{3,1,0,2:T(2,128)(2,1)}), bf16[1,2,128,128]{3,1,0,2:T(2,128)(2,1)S(1)}, u32[]{:S(2)}, u32[]{:S(2)}) async-start(bf16[1,2,128,128]{3,1,0,2:T(2,128)(2,1)} %bitcast.42), calls=%async_computation.1 | async-start | bytes 131072 | tf_op jit(solution)/shard_map/all_to_all | solution.py:80
  164.5 0.0 copy-done.1
  164.5 0.1 copy.48
  164.6 9.9 %all-to-all-done.1 = bf16[1,2,128,128]{3,1,0,2:T(2,128)(2,1)S(1)} async-done(((bf16[1,2,128,128]{3,1,0,2:T(2,128)(2,1)}), bf16[1,2,128,128]{3,1,0,2:T(2,128)(2,1)S(1)}, u32[]{:S(2)}, u32[]{:S(2)}) %all-to-all-start.1) | async-done | bytes 65568 | tf_op jit(solution)/shard_map/all_to_all | solution.py:80
  174.5 0.1 copy.62
  174.6 0.4 fusion.7
  175.1 0.4 fusion.6
  175.5 0.4 fusion.13
  176.0 0.8 copy.66
  (7 shorter events, 0.2 us)
Async XLA Ops:
  0.0 79.0 %copy-start = (bf16[3,128,128]{2,1,0:T(8,128)(2,1)S(1)}, bf16[3,128,128]{2,1,0:T(8,128)(2,1)}, u32[]{:S(2)}) copy-start(bf16[3,128,128]{2,1,0:T(8,128)(2,1)} %param.11) | copy-start | bytes 294916
  4.5 25.5 %all-to-all-start = ((bf16[1,128,2,128]{3,2,0,1:T(2,128)(2,1)}), bf16[1,128,2,128]{3,2,0,1:T(2,128)(2,1)S(1)}, u32[]{:S(2)}, u32[]{:S(2)}) async-start(bf16[1,128,2,128]{3,2,0,1:T(2,128)(2,1)} %copy.52), calls=%async_computation | async-start | bytes 131072 | tf_op jit(solution)/shard_map/all_to_all | solution.py:46
  125.5 39.0 %copy-start.1 = (bf16[1,2,128,128]{3,2,1,0:T(8,128)(2,1)S(1)}, bf16[1,2,128,128]{3,2,1,0:T(8,128)(2,1)}, u32[]{:S(2)}) copy-start(bf16[1,2,128,128]{3,2,1,0:T(8,128)(2,1)} %param.9) | copy-start | bytes 196612
  146.5 28.0 %all-to-all-start.1 = ((bf16[1,2,128,128]{3,1,0,2:T(2,128)(2,1)}), bf16[1,2,128,128]{3,1,0,2:T(2,128)(2,1)S(1)}, u32[]{:S(2)}, u32[]{:S(2)}) async-start(bf16[1,2,128,128]{3,1,0,2:T(2,128)(2,1)} %bitcast.42), calls=%async_computation.1 | async-start | bytes 131072 | tf_op jit(solution)/shard_map/all_to_all | solution.py:80
where the time goes:
time: 178 us; the launch traced here: 177 us
  blocking collectives  48.8 us (27%)
  other arithmetic  45.3 us (25%)
  starting transfers between devices  33.4 us (19%)
  local copies, waits for them, and re-layouts  31.9 us (18%)
  waiting for transfers between devices  11.1 us (6%)
  matrix products  5.42 us (3%)
    psum x1, blocking collectives, local(): member_total = lax.psum(partial_total, 'narrow')  48.8 us
    unnamed x4, other arithmetic  34.1 us
    all_to_all x1, starting transfers between devices, local(): lax.all_to_all(column_grad, 'wide', split_axis=2, concat_axis=1, tiled=True)  18 us
    all_to_all x1, starting transfers between devices, local(): lax.all_to_all(localized, 'wide', split_axis=1, concat_axis=2, tiled=True)  15.4 us
    transpose x1, local copies, waits for them, and re-layouts, local(): jnp.einsum('vlk,viky->vily', vertical, member_total.astype(jnp.bfloat16),...  13.7 us
    convert_element_type x1, local copies, waits for them, and re-layouts, local(): obs_adjoint = spread_back.astype(jnp.bfloat16)  11.1 us
    all_to_all x1, waiting for transfers between devices, local(): lax.all_to_all(column_grad, 'wide', split_axis=2, concat_axis=1, tiled=True)  9.9 us
    convert_element_type x1, other arithmetic, local(): obs_adjoint = spread_back.astype(jnp.bfloat16)  8.93 us
  transfers between devices with their start and end apart: 2, of which 2 were waited for; matrix products, arithmetic and copies ran while one was open for 5% of the time, Pallas kernels for 0%

commit v1 on v0

v1 whole, which is shorter than its diff:
```python
import functools

import jax
import jax.numpy as jnp
import ml_dtypes
import numpy as np
from jax import lax
from jax.experimental import pallas as pl
from jax.experimental.pallas import tpu as pltpu
from jax.sharding import PartitionSpec as P

MESH = pl.DeviceIdType.MESH
scale_lengths = (1.5, 4.0, 12.0)
scale_mix = (0.6, 0.5, 0.4)
bf16, f32 = jnp.bfloat16, jnp.float32


def gauss_table(length, spread):
    places = np.arange(length).astype(np.float32)
    offset = places[:, None] - places[None, :]
    norm_factor = np.sqrt(np.sqrt(np.float32(np.pi)) * np.float32(spread))
    values = np.exp(np.float32(-0.5) * offset * offset / np.float32(spread * spread)) / norm_factor
    values = np.where(np.abs(offset) <= 4.0 * spread, values, np.float32(0.0))
    return values.astype(ml_dtypes.bfloat16)


def row_table(table, blocks, levels):
    length = table.shape[0]
    rows = length // blocks
    wide = np.zeros((rows, blocks, levels, levels, length), ml_dtypes.bfloat16)
    by_row = table.reshape(blocks, rows, length).transpose(1, 0, 2)
    for level in range(levels):
        wide[:, :, level, level, :] = by_row
    return wide.reshape(rows * blocks * levels, levels * length)


def dot(a, b):
    return jnp.dot(a, b, preferred_element_type=f32)


def kernel(
    nw, nn,
    weights_ref, perturb_ref, vertical_ref, to_rows_ref, to_levels_ref, table_ref,
    column_ref, level_ref, count_ref, flag_ref, value_ref, weight_ref,
    out_ref,
    send_a, recv_a, at_mine, at_all, send_b, recv_b, pick, pick_t, spread, vertical_t,
    send_sem, recv_sem, at_send_sem, at_recv_sem,
):
    me = lax.axis_index("wide")
    member = lax.axis_index("narrow")
    rows, blocks, levels, width = send_a.shape
    num_vars, num_levels, _ = vertical_ref.shape
    slot_rows = column_ref.shape[0]
    slots = slot_rows * 128
    cells = rows * width

    barrier = pltpu.get_barrier_semaphore()

    def greet(k, carry):
        peer = lax.rem(me + k, nw)
        pl.semaphore_signal(barrier, inc=1, device_id={"wide": peer}, device_id_type=MESH)
        return carry

    lax.fori_loop(1, nw, greet, 0)
    for k in range(1, nn):
        pl.semaphore_signal(
            barrier, inc=1, device_id={"narrow": lax.rem(member + k, nn)}, device_id_type=MESH
        )

    def exchange(source, target, phase):
        own = pltpu.make_async_copy(source.at[:, me], target.at[:, me], recv_sem.at[phase])
        own.start()

        def put(k, carry):
            peer = lax.rem(me + k, nw)
            pltpu.make_async_remote_copy(
                src_ref=source.at[:, peer],
                dst_ref=target.at[:, me],
                send_sem=send_sem.at[phase],
                recv_sem=recv_sem.at[phase],
                device_id={"wide": peer},
                device_id_type=MESH,
            ).start()
            return carry

        lax.fori_loop(1, nw, put, 0)

    def arrived(target, phase):
        pltpu.make_async_copy(target, target, recv_sem.at[phase]).wait()

    def departed(source, phase):
        part = source.at[:, pl.ds(0, nw - 1)]
        pltpu.make_async_copy(part, part, send_sem.at[phase]).wait()

    own_weights = weights_ref[...]
    localized = None
    for s, mix in enumerate(scale_mix):
        across = dot(to_rows_ref[s], own_weights).astype(bf16)
        scaled = mix * dot(across, table_ref[s])
        localized = scaled if localized is None else localized + scaled
    send_a[...] = localized.astype(bf16).reshape(send_a.shape)
    pl.semaphore_wait(barrier, nw - 1 + nn - 1)
    exchange(send_a, recv_a, 0)

    cell_of = lax.broadcasted_iota(jnp.int32, (cells, 128), 0)
    cell_of_t = lax.broadcasted_iota(jnp.int32, (128, cells), 1)
    columns = column_ref[...]
    columns_t = jnp.transpose(columns)
    for r in range(slot_rows):
        part = slice(r * 128, (r + 1) * 128)
        pick[:, part] = jnp.where(cell_of == columns[r : r + 1, :], 1.0, 0.0).astype(bf16)
        pick_t[part, :] = jnp.where(cell_of_t == columns_t[:, r : r + 1], 1.0, 0.0).astype(bf16)
    for v in range(num_vars):
        vertical_t[v] = jnp.transpose(vertical_ref[v].astype(f32)).astype(bf16)

    arrived(recv_a, 0)
    held = [recv_a[i].reshape(num_levels, width).astype(f32) for i in range(rows)]
    increment = []
    for v in range(num_vars):
        product = jnp.concatenate(
            [(perturb_ref[v * rows + i].astype(f32) * held[i]).astype(bf16) for i in range(rows)], axis=1
        )
        increment.append(dot(vertical_ref[v], product).astype(bf16))
    increment = jnp.concatenate(increment, axis=0)

    step = 256
    level_of = lax.broadcasted_iota(jnp.int32, (num_levels, 128), 0)
    for t in range(slots // step):
        met = dot(increment, pick[:, t * step : (t + 1) * step])
        for h in range(step // 128):
            r = t * (step // 128) + h
            here = level_of == level_ref[r : r + 1, :]
            for v in range(num_vars):
                block = met[v * num_levels : (v + 1) * num_levels, h * 128 : (h + 1) * 128]
                summed = jnp.sum(jnp.where(here, block, 0.0), axis=0, keepdims=True)
                at_mine[v, r : r + 1, :] = summed.astype(bf16)

    copies = []
    for k in range(1, nn):
        peer = lax.rem(member + k, nn)
        copy = pltpu.make_async_remote_copy(
            src_ref=at_mine,
            dst_ref=at_all.at[member],
            send_sem=at_send_sem,
            recv_sem=at_recv_sem,
            device_id={"narrow": peer},
            device_id_type=MESH,
        )
        copy.start()
        copies.append(copy)
    own = pltpu.make_async_copy(at_mine, at_all.at[member], at_recv_sem)
    own.start()
    pltpu.make_async_copy(at_all, at_all, at_recv_sem).wait()

    slot_of = lax.broadcasted_iota(jnp.int32, (slot_rows, 128), 0) * 128 + lax.broadcasted_iota(
        jnp.int32, (slot_rows, 128), 1
    )
    live = (slot_of < count_ref[0]) & (flag_ref[...] > 0)
    for v in range(num_vars):
        at_obs = at_all[0, v].astype(f32)
        for k in range(1, nn):
            at_obs = at_obs + at_all[k, v].astype(f32)
        misfit = jnp.where(live, weight_ref[v] * (at_obs - value_ref[v]), 0.0)
        for r in range(slot_rows):
            here = level_of == level_ref[r : r + 1, :]
            spread[v * num_levels : (v + 1) * num_levels, r * 128 : (r + 1) * 128] = jnp.where(
                here, misfit[r : r + 1, :], 0.0
            ).astype(bf16)
    adjoint = dot(spread[...], pick_t[...]).astype(bf16)

    sums = [None] * rows
    for v in range(num_vars):
        lifted = dot(vertical_t[v], adjoint[v * num_levels : (v + 1) * num_levels]).astype(bf16).astype(f32)
        for i in range(rows):
            term = perturb_ref[v * rows + i].astype(f32) * lifted[:, i * width : (i + 1) * width]
            sums[i] = term if sums[i] is None else sums[i] + term
    for i in range(rows):
        send_b[i] = sums[i].astype(bf16).reshape(send_b.shape[1:])
    exchange(send_b, recv_b, 1)
    arrived(recv_b, 1)

    level_grad = recv_b[...].reshape(rows * blocks * levels, width)
    gradient = own_weights.astype(f32)
    for s, mix in enumerate(scale_mix):
        back = dot(level_grad, table_ref[s]).astype(bf16)
        gradient = gradient + mix * dot(to_levels_ref[s], back)
    out_ref[...] = gradient

    departed(send_a, 0)
    departed(send_b, 1)
    pltpu.make_async_copy(at_all.at[pl.ds(0, nn - 1)], at_all.at[pl.ds(0, nn - 1)], at_send_sem).wait()


def solution(mesh):
    nw, nn = mesh.shape["wide"], mesh.shape["narrow"]

    def local(weights, perturb, vertical, obs_column, obs_level, obs_count, flag, obs_value, obs_weight):
        _, levels, length, width = weights.shape
        _, num_vars, rows, num_levels, _ = perturb.shape
        slots = obs_column.shape[0]
        slot_rows = slots // 128
        tables = [gauss_table(length, spread) for spread in scale_lengths]
        to_rows = np.stack([row_table(table, nw, levels) for table in tables])
        to_levels = np.ascontiguousarray(to_rows.transpose(0, 2, 1))
        chunk = pltpu.VMEM((rows, nw, levels, width), bf16)
        vmem = pl.BlockSpec(memory_space=pltpu.VMEM)
        smem = pl.BlockSpec(memory_space=pltpu.SMEM)
        out = pl.pallas_call(
            functools.partial(kernel, nw, nn),
            out_shape=jax.ShapeDtypeStruct((levels * length, width), f32),
            in_specs=[vmem] * 8 + [smem] + [vmem] * 3,
            out_specs=vmem,
            scratch_shapes=[
                chunk,
                chunk,
                pltpu.VMEM((num_vars, slot_rows, 128), bf16),
                pltpu.VMEM((nn, num_vars, slot_rows, 128), bf16),
                chunk,
                chunk,
                pltpu.VMEM((rows * width, slots), bf16),
                pltpu.VMEM((slots, rows * width), bf16),
                pltpu.VMEM((num_vars * num_levels, slots), bf16),
                pltpu.VMEM((num_vars, num_levels, num_levels), bf16),
                pltpu.SemaphoreType.DMA((2,)),
                pltpu.SemaphoreType.DMA((2,)),
                pltpu.SemaphoreType.DMA,
                pltpu.SemaphoreType.DMA,
            ],
            compiler_params=pltpu.CompilerParams(
                collective_id=0, has_side_effects=True, vmem_limit_bytes=48 * 1024 * 1024
            ),
        )(
            weights.reshape(levels * length, width),
            perturb.reshape(num_vars * rows, num_levels, width),
            vertical,
            jnp.asarray(to_rows),
            jnp.asarray(to_levels),
            jnp.asarray(np.stack(tables)),
            obs_column.reshape(slot_rows, 128),
            obs_level.reshape(slot_rows, 128),
            obs_count,
            flag.reshape(slot_rows, 128),
            obs_value.reshape(num_vars, slot_rows, 128),
            obs_weight.reshape(num_vars, slot_rows, 128),
        )
        return out.reshape(weights.shape)

    placed = (
        P("narrow", "wide", None, None),
        P("narrow", None, "wide", None, None),
        P(),
        P("wide"),
        P("wide"),
        P("wide"),
        P("wide"),
        P(None, "wide"),
        P(None, "wide"),
    )
    return jax.shard_map(
        local,
        mesh=mesh,
        in_specs=placed,
        out_specs=P("narrow", "wide", None, None),
        check_vma=False,
    )
```

time: 178 us -> 45.2 us (0.25)
  blocking collectives: 48.8 us -> 0 us
  other arithmetic: 45.3 us -> 0 us
  Pallas kernels: 0 us -> 38 us
  starting transfers between devices: 33.4 us -> 0 us
  local copies, waits for them, and re-layouts: 31.9 us -> 6.11 us
  waiting for transfers between devices: 11.1 us -> 0 us
  matrix products: 5.42 us -> 0 us
    psum x1 -> x0, blocking collectives: 48.8 us -> none  [local(): member_total = lax.psum(partial_total, 'narrow')]
    pallas_call x0 -> x1, Pallas kernels: none -> 38 us  [local(): pl.pallas_call(functools.partial(kernel, nw, nn), out_shape=jax.ShapeDtyp...]
    unnamed x4 -> x0, other arithmetic: 34.1 us -> none
    all_to_all x2 -> x0, starting transfers between devices: 33.4 us -> none  [the longest x1 18 us: local(): lax.all_to_all(column_grad, 'wide', split_axis=2, concat_axis=1, tiled=True)]
    transpose x1 -> x0, local copies, waits for them, and re-layouts: 13.7 us -> none  [local(): jnp.einsum('vlk,viky->vily', vertical, member_total.astype(jnp.bfloat16),...]
    convert_element_type x2 -> x0, local copies, waits for them, and re-layouts: 11.9 us -> none  [the longest x1 11.1 us: local(): obs_adjoint = spread_back.astype(jnp.bfloat16)]
    all_to_all x2 -> x0, waiting for transfers between devices: 11.1 us -> none  [the longest x1 9.9 us: local(): lax.all_to_all(column_grad, 'wide', split_axis=2, concat_axis=1, tiled=True)]
    convert_element_type x2 -> x0, other arithmetic: 8.93 us -> none  [the longest x1 8.93 us: local(): obs_adjoint = spread_back.astype(jnp.bfloat16)]
  transfers between devices with their start and end apart: 2 -> 0, of which waited for: 2 -> 0; matrix products, arithmetic and copies ran while one was open for 5% -> 0% of each run, Pallas kernels for 0% -> 0%
where the time goes in v1:
time: 45.2 us; the launch traced here: 44.9 us
  Pallas kernels  38 us (84%)
  local copies, waits for them, and re-layouts  6.11 us (14%)
  between operations  0.75 us (2%)
    pallas_call x1, Pallas kernels, local(): pl.pallas_call(functools.partial(kernel, nw, nn), out_shape=jax.ShapeDtyp...  38 us
    unnamed x19, local copies, waits for them, and re-layouts  5.32 us

profile of v1, /device:TPU:1, one launch (start us, length us, event | category | flops | bytes accessed | tf_op | source)
XLA Modules:
  0.0 44.9 jit_solution(42494016660806966)
XLA Ops:
  0.0 0.0 copy-start.3
  0.7 0.0 copy-start.6
  0.7 0.0 copy-start.7
  0.7 0.0 copy-start.8
  0.7 0.8 %copy_bitcast_fusion = (f32[3,16,128]{2,1,0:T(8,128)S(1)}, f32[3,16,128]{2,1,0:T(8,128)S(1)}) fusion(f32[1,3,16,128]{3,1,2,0:T(4,128)} %bitcast.18, f32[1,3,16,128]{3,1,2,0:T(4,128)} %bitcast.19), kind=kLoop, calls=%fused_computation | loop fusion | bytes 98304 | tf_op jit(solution)/shard_map/reshape | solution.py:244
  1.5 0.0 copy-done.3
  1.5 0.0 copy-done.6
  1.5 0.0 copy-done.7
  1.5 0.0 copy-done.8
  1.5 0.0 copy-start
  1.6 1.0 %copy-done = bf16[3,256,256]{2,1,0:T(8,128)(2,1)S(1)} copy-done((bf16[3,256,256]{2,1,0:T(8,128)(2,1)S(1)}, bf16[3,256,256]{2,1,0:T(8,128)(2,1)}, u32[]{:S(2)}) %copy-start) | copy-done | bytes 393240
  2.5 0.0 copy-start.1
  2.5 1.0 %copy-done.1 = bf16[3,256,256]{2,1,0:T(8,128)(2,1)S(1)} copy-done((bf16[3,256,256]{2,1,0:T(8,128)(2,1)S(1)}, bf16[3,256,256]{2,1,0:T(8,128)(2,1)}, u32[]{:S(2)}) %copy-start.1) | copy-done | bytes 393240
  3.5 0.0 copy-start.2
  3.5 0.9 %copy-done.2 = bf16[1,3,2,128,128]{4,3,2,1,0:T(8,128)(2,1)S(1)} copy-done((bf16[1,3,2,128,128]{4,3,2,1,0:T(8,128)(2,1)S(1)}, bf16[1,3,2,128,128]{4,3,2,1,0:T(8,128)(2,1)}, u32[]{:S(2)}) %copy-start.2) | copy-done | bytes 196632
  4.5 0.0 copy-start.4
  4.5 0.9 %copy-done.4 = bf16[3,128,128]{2,1,0:T(8,128)(2,1)S(1)} copy-done((bf16[3,128,128]{2,1,0:T(8,128)(2,1)S(1)}, bf16[3,128,128]{2,1,0:T(8,128)(2,1)}, u32[]{:S(2)}) %copy-start.4) | copy-done | bytes 98328
  5.4 0.0 copy-start.5
  5.4 0.8 %copy-done.5 = bf16[1,2,128,128]{3,2,1,0:T(8,128)(2,1)S(1)} copy-done((bf16[1,2,128,128]{3,2,1,0:T(8,128)(2,1)S(1)}, bf16[1,2,128,128]{3,2,1,0:T(8,128)(2,1)}, u32[]{:S(2)}) %copy-start.5) | copy-done | bytes 65560
  6.2 38.0 %shard_map.118 = f32[256,128]{1,0:T(8,128)S(1)} custom-call(bf16[256,128]{1,0:T(8,128)(2,1)S(1)} %bitcast.14, bf16[6,128,128]{2,1,0:T(8,128)(2,1)S(1)} %bitcast.13, bf16[3,128,128]{2,1,0:T(8,128)(2,1)S(1)} %copy-done.3, bf16[3,256,256]{2,1,0:T(8,128)(2,1)S(1)} %copy-done.1, bf16[3,256,256]{2,1,0:T(8,128)(2,1)S(1)} %copy-done, ...), custom_call_target="tpu_custom_call" | custom-call | tf_op jit(solution)/shard_map/pallas_call | solution.py:208
  44.2 0.7 %copy.19 = f32[1,2,128,128]{3,2,1,0:T(8,128)} copy(f32[1,2,128,128]{3,2,1,0:T(8,128)S(1)} %bitcast.12) | data formatting | bytes 262144
Async XLA Ops:
  0.0 1.5 %copy-start.3 = (bf16[3,128,128]{2,1,0:T(8,128)(2,1)S(1)}, bf16[3,128,128]{2,1,0:T(8,128)(2,1)}, u32[]{:S(2)}) copy-start(bf16[3,128,128]{2,1,0:T(8,128)(2,1)} %vertical_ref.1) | copy-start | bytes 294916
  0.7 0.8 %copy-start.6 = (s32[2048]{0:T(1024)S(1)}, s32[2048]{0:T(1024)}, u32[]{:S(2)}) copy-start(s32[2048]{0:T(1024)} %param.15) | copy-start | bytes 24580
  0.7 0.8 %copy-start.7 = (s32[2048]{0:T(1024)S(1)}, s32[2048]{0:T(1024)}, u32[]{:S(2)}) copy-start(s32[2048]{0:T(1024)} %param.16) | copy-start | bytes 24580
  0.7 0.8 %copy-start.8 = (s32[2048]{0:T(1024)S(1)}, s32[2048]{0:T(1024)}, u32[]{:S(2)}) copy-start(s32[2048]{0:T(1024)} %param.18) | copy-start | bytes 24580
  1.5 1.0 %copy-start = (bf16[3,256,256]{2,1,0:T(8,128)(2,1)S(1)}, bf16[3,256,256]{2,1,0:T(8,128)(2,1)}, u32[]{:S(2)}) copy-start(bf16[3,256,256]{2,1,0:T(8,128)(2,1)} %constant.7.clone.to_levels_ref) | copy-start | bytes 1179652
  2.5 1.0 %copy-start.1 = (bf16[3,256,256]{2,1,0:T(8,128)(2,1)S(1)}, bf16[3,256,256]{2,1,0:T(8,128)(2,1)}, u32[]{:S(2)}) copy-start(bf16[3,256,256]{2,1,0:T(8,128)(2,1)} %constant.6.clone.to_rows_ref) | copy-start | bytes 1179652
  3.5 0.9 %copy-start.2 = (bf16[1,3,2,128,128]{4,3,2,1,0:T(8,128)(2,1)S(1)}, bf16[1,3,2,128,128]{4,3,2,1,0:T(8,128)(2,1)}, u32[]{:S(2)}) copy-start(bf16[1,3,2,128,128]{4,3,2,1,0:T(8,128)(2,1)} %param.13) | copy-start | bytes 589828
  4.5 0.9 %copy-start.4 = (bf16[3,128,128]{2,1,0:T(8,128)(2,1)S(1)}, bf16[3,128,128]{2,1,0:T(8,128)(2,1)}, u32[]{:S(2)}) copy-start(bf16[3,128,128]{2,1,0:T(8,128)(2,1)} %constant.8.clone.table_ref) | copy-start | bytes 294916
  5.4 0.8 %copy-start.5 = (bf16[1,2,128,128]{3,2,1,0:T(8,128)(2,1)S(1)}, bf16[1,2,128,128]{3,2,1,0:T(8,128)(2,1)}, u32[]{:S(2)}) copy-start(bf16[1,2,128,128]{3,2,1,0:T(8,128)(2,1)} %param.12) | copy-start | bytes 196612

commit v2 on v1

--- a/solution.py
+++ b/solution.py
@@ -12,6 +12,7 @@
 MESH = pl.DeviceIdType.MESH
 scale_lengths = (1.5, 4.0, 12.0)
 scale_mix = (0.6, 0.5, 0.4)
+NUM_LOADS = 12
 bf16, f32 = jnp.bfloat16, jnp.float32
 
 
@@ -40,12 +41,22 @@
 
 def kernel(
     nw, nn,
-    weights_ref, perturb_ref, vertical_ref, to_rows_ref, to_levels_ref, table_ref,
-    column_ref, level_ref, count_ref, flag_ref, value_ref, weight_ref,
-    out_ref,
-    send_a, recv_a, at_mine, at_all, send_b, recv_b, pick, pick_t, spread, vertical_t,
+    *refs,
+):
+    sources, out_ref = refs[:NUM_LOADS], refs[NUM_LOADS]
+    loaded = refs[NUM_LOADS + 1 : 2 * NUM_LOADS + 1]
+    (
+        weights_ref, to_rows_ref, table_ref, column_ref, level_ref, vertical_ref,
+        perturb_ref, flag_ref, value_ref, weight_ref, count_ref, to_levels_ref,
+    ) = loaded
+    (
+        load_sem, send_a, recv_a, at_mine, at_all, send_b, recv_b, pick, pick_t, spread, vertical_t,
     send_sem, recv_sem, at_send_sem, at_recv_sem,
-):
+    ) = refs[2 * NUM_LOADS + 1 :]
+    loads = [pltpu.make_async_copy(a, b, load_sem.at[n]) for n, (a, b) in enumerate(zip(sources, loaded))]
+    for load in loads:
+        load.start()
+
     me = lax.axis_index("wide")
     member = lax.axis_index("narrow")
     rows, blocks, levels, width = send_a.shape
@@ -92,6 +103,9 @@
         part = source.at[:, pl.ds(0, nw - 1)]
         pltpu.make_async_copy(part, part, send_sem.at[phase]).wait()
 
+    for load in loads[:3]:
+        load.wait()
+
     own_weights = weights_ref[...]
     localized = None
     for s, mix in enumerate(scale_mix):
@@ -102,6 +116,9 @@
     pl.semaphore_wait(barrier, nw - 1 + nn - 1)
     exchange(send_a, recv_a, 0)
 
+    for load in loads[3:6]:
+        load.wait()
+
     cell_of = lax.broadcasted_iota(jnp.int32, (cells, 128), 0)
     cell_of_t = lax.broadcasted_iota(jnp.int32, (128, cells), 1)
     columns = column_ref[...]
@@ -112,6 +129,9 @@
         pick_t[part, :] = jnp.where(cell_of_t == columns_t[:, r : r + 1], 1.0, 0.0).astype(bf16)
     for v in range(num_vars):
         vertical_t[v] = jnp.transpose(vertical_ref[v].astype(f32)).astype(bf16)
+
+    for load in loads[6:]:
+        load.wait()
 
     arrived(recv_a, 0)
     held = [recv_a[i].reshape(num_levels, width).astype(f32) for i in range(rows)]
@@ -155,17 +175,20 @@
     slot_of = lax.broadcasted_iota(jnp.int32, (slot_rows, 128), 0) * 128 + lax.broadcasted_iota(
         jnp.int32, (slot_rows, 128), 1
     )
-    live = (slot_of < count_ref[0]) & (flag_ref[...] > 0)
+    live = jnp.where((slot_of < count_ref[0]) & (flag_ref[...] > 0), 1.0, 0.0)
     for v in range(num_vars):
         at_obs = at_all[0, v].astype(f32)
         for k in range(1, nn):
             at_obs = at_obs + at_all[k, v].astype(f32)
-        misfit = jnp.where(live, weight_ref[v] * (at_obs - value_ref[v]), 0.0)
         for r in range(slot_rows):
+            part = slice(r * 128, (r + 1) * 128)
+            misfit = jnp.where(
+                live[r : r + 1] > 0.0,
+                weight_ref[v : v + 1, part] * (at_obs[r : r + 1] - value_ref[v : v + 1, part]),
+                0.0,
+            )
             here = level_of == level_ref[r : r + 1, :]
-            spread[v * num_levels : (v + 1) * num_levels, r * 128 : (r + 1) * 128] = jnp.where(
-                here, misfit[r : r + 1, :], 0.0
-            ).astype(bf16)
+            spread[v * num_levels : (v + 1) * num_levels, part] = jnp.where(here, misfit, 0.0).astype(bf16)
     adjoint = dot(spread[...], pick_t[...]).astype(bf16)
 
     sums = [None] * rows
@@ -202,15 +225,33 @@
         tables = [gauss_table(length, spread) for spread in scale_lengths]
         to_rows = np.stack([row_table(table, nw, levels) for table in tables])
         to_levels = np.ascontiguousarray(to_rows.transpose(0, 2, 1))
+        operands = (
+            weights.reshape(levels * length, width),
+            jnp.asarray(to_rows),
+            jnp.asarray(np.stack(tables)),
+            obs_column.reshape(slot_rows, 128),
+            obs_level.reshape(slot_rows, 128),
+            vertical,
+            perturb.reshape(num_vars * rows, num_levels, width),
+            flag.reshape(slot_rows, 128),
+            obs_value,
+            obs_weight,
+            obs_count,
+            jnp.asarray(to_levels),
+        )
         chunk = pltpu.VMEM((rows, nw, levels, width), bf16)
         vmem = pl.BlockSpec(memory_space=pltpu.VMEM)
-        smem = pl.BlockSpec(memory_space=pltpu.SMEM)
         out = pl.pallas_call(
             functools.partial(kernel, nw, nn),
             out_shape=jax.ShapeDtypeStruct((levels * length, width), f32),
-            in_specs=[vmem] * 8 + [smem] + [vmem] * 3,
+            in_specs=[pl.BlockSpec(memory_space=pltpu.HBM)] * NUM_LOADS,
             out_specs=vmem,
             scratch_shapes=[
+                (pltpu.SMEM if operand is obs_count else pltpu.VMEM)(operand.shape, operand.dtype)
+                for operand in operands
+            ]
+            + [
+                pltpu.SemaphoreType.DMA((NUM_LOADS,)),
                 chunk,
                 chunk,
                 pltpu.VMEM((num_vars, slot_rows, 128), bf16),
@@ -227,22 +268,9 @@
                 pltpu.SemaphoreType.DMA,
             ],
             compiler_params=pltpu.CompilerParams(
-                collective_id=0, has_side_effects=True, vmem_limit_bytes=48 * 1024 * 1024
+                collective_id=0, has_side_effects=True, vmem_limit_bytes=60 * 1024 * 1024
             ),
-        )(
-            weights.reshape(levels * length, width),
-            perturb.reshape(num_vars * rows, num_levels, width),
-            vertical,
-            jnp.asarray(to_rows),
-            jnp.asarray(to_levels),
-            jnp.asarray(np.stack(tables)),
-            obs_column.reshape(slot_rows, 128),
-            obs_level.reshape(slot_rows, 128),
-            obs_count,
-            flag.reshape(slot_rows, 128),
-            obs_value.reshape(num_vars, slot_rows, 128),
-            obs_weight.reshape(num_vars, slot_rows, 128),
-        )
+        )(*operands)
         return out.reshape(weights.shape)
 
     placed = (

time: 45.2 us -> 41 us (0.907)
  local copies, waits for them, and re-layouts: 6.11 us -> 1.57 us
  Pallas kernels: 38 us -> 38.7 us
    unnamed x19 -> x1, local copies, waits for them, and re-layouts: 5.32 us -> 1.57 us
    reshape x1 -> x0, local copies, waits for them, and re-layouts: 0.8 us -> none  [local(): obs_weight.reshape(num_vars, slot_rows, 128)]
    pallas_call x1, Pallas kernels: 38 us -> 38.7 us  [local(): pl.pallas_call(functools.partial(kernel, nw, nn), out_shape=jax.ShapeDtyp...]
where the time goes in v2:
time: 41 us; the launch traced here: 40.9 us
  Pallas kernels  38.7 us (94%)
  local copies, waits for them, and re-layouts  1.57 us (4%)
  between operations  0.66 us (2%)
    pallas_call x1, Pallas kernels, local(): pl.pallas_call(functools.partial(kernel, nw, nn), out_shape=jax.ShapeDtyp...  38.7 us
    unnamed x1, local copies, waits for them, and re-layouts  1.57 us

profile of v2, /device:TPU:1, one launch (start us, length us, event | category | flops | bytes accessed | tf_op | source)
XLA Modules:
  0.0 40.9 jit_solution(5363329092636044833)
XLA Ops:
  0.7 38.7 %shard_map.118 = f32[256,128]{1,0:T(8,128)} custom-call(bf16[256,128]{1,0:T(8,128)(2,1)} %bitcast.8, bf16[3,256,256]{2,1,0:T(8,128)(2,1)} %constant.6.clone.refs_1_, bf16[3,128,128]{2,1,0:T(8,128)(2,1)} %constant.7.clone.refs_2_, s32[16,128]{1,0:T(8,128)} %bitcast.9, s32[16,128]{1,0:T(8,128)} %bitcast.10, bf16[3,128,128]{2,1,0:T(8,128)(2,1)} %refs_5_.1, ...), custom_call_target="tpu_custom_call" | custom-call | tf_op jit(solution)/shard_map/pallas_call | solution.py:244
  39.3 1.6 %copy.15 = f32[1,2,128,128]{3,2,1,0:T(8,128)} copy(f32[1,2,128,128]{3,2,1,0:T(8,128)} %bitcast.6) | data formatting | bytes 262144

commit v3 on v2

v3 whole, which is shorter than its diff:
```python
import functools

import jax
import jax.numpy as jnp
import ml_dtypes
import numpy as np
from jax import lax
from jax.experimental import pallas as pl
from jax.experimental.pallas import tpu as pltpu
from jax.sharding import PartitionSpec as P

MESH = pl.DeviceIdType.MESH
scale_lengths = (1.5, 4.0, 12.0)
scale_mix = (0.6, 0.5, 0.4)
NUM_LOADS = 11
NARROW_FAR_FIRST = (6, 2, 5, 3, 4, 7, 1)
FAR_FIRST = sorted(range(1, 64), key=lambda k: -min(k, 64 - k))
bf16, f32 = jnp.bfloat16, jnp.float32


def gauss_table(length, spread):
    places = np.arange(length).astype(np.float32)
    offset = places[:, None] - places[None, :]
    norm_factor = np.sqrt(np.sqrt(np.float32(np.pi)) * np.float32(spread))
    values = np.exp(np.float32(-0.5) * offset * offset / np.float32(spread * spread)) / norm_factor
    values = np.where(np.abs(offset) <= 4.0 * spread, values, np.float32(0.0))
    return values.astype(ml_dtypes.bfloat16)


def row_table(table, blocks, levels):
    length = table.shape[0]
    rows = length // blocks
    wide = np.zeros((rows, blocks, levels, levels, length), ml_dtypes.bfloat16)
    by_row = table.reshape(blocks, rows, length).transpose(1, 0, 2)
    for level in range(levels):
        wide[:, :, level, level, :] = by_row
    return wide.reshape(rows * blocks * levels, levels * length)


def dot(a, b):
    return jnp.dot(a, b, preferred_element_type=f32)


def kernel(
    nw, nn,
    count_ref, *refs,
):
    sources, out_ref = refs[:NUM_LOADS], refs[NUM_LOADS]
    loaded = refs[NUM_LOADS + 1 : 2 * NUM_LOADS + 1]
    (
        weights_ref, to_rows_ref, table_ref, column_ref, level_ref, vertical_ref,
        perturb_ref, flag_ref, value_ref, weight_ref, to_levels_ref,
    ) = loaded
    (
        load_sem, send_a, recv_a, at_row, at_mine, at_all, send_b, recv_b, pick, pick_t, spread, vertical_t,
        at_level, value_rows, weight_rows,
    send_sem, recv_sem, at_send_sem, at_recv_sem,
    ) = refs[2 * NUM_LOADS + 1 :]
    me = lax.axis_index("wide")
    member = lax.axis_index("narrow")
    rows, blocks, levels, width = send_a.shape
    num_vars, num_levels, _ = vertical_ref.shape
    slot_rows = column_ref.shape[0]
    slots = slot_rows * 128
    cells = rows * width

    barrier = pltpu.get_barrier_semaphore()

    for far in FAR_FIRST:
        peer = lax.rem(me + far, nw)
        pl.semaphore_signal(barrier, inc=1, device_id={"wide": peer}, device_id_type=MESH)
    for k in range(1, nn):
        pl.semaphore_signal(
            barrier, inc=1, device_id={"narrow": lax.rem(member + k, nn)}, device_id_type=MESH
        )

    loads = [pltpu.make_async_copy(a, b, load_sem.at[n]) for n, (a, b) in enumerate(zip(sources, loaded))]
    for load in loads:
        load.start()

    def exchange(source, target, phase):
        own = pltpu.make_async_copy(source.at[:, me], target.at[:, me], recv_sem.at[phase])
        own.start()

        for far in FAR_FIRST:
            peer = lax.rem(me + far, nw)
            pltpu.make_async_remote_copy(
                src_ref=source.at[:, peer],
                dst_ref=target.at[:, me],
                send_sem=send_sem.at[phase],
                recv_sem=recv_sem.at[phase],
                device_id={"wide": peer},
                device_id_type=MESH,
            ).start()

    def arrived(target, phase):
        pltpu.make_async_copy(target, target, recv_sem.at[phase]).wait()

    def departed(source, phase):
        part = source.at[:, pl.ds(0, nw - 1)]
        pltpu.make_async_copy(part, part, send_sem.at[phase]).wait()

    for load in loads[:3]:
        load.wait()

    own_weights = weights_ref[...]
    localized = None
    for s, mix in enumerate(scale_mix):
        across = dot(to_rows_ref[s], own_weights).astype(bf16)
        scaled = mix * dot(across, table_ref[s])
        localized = scaled if localized is None else localized + scaled
    send_a[...] = localized.astype(bf16).reshape(send_a.shape)
    pl.semaphore_wait(barrier, nw - 1 + nn - 1)
    exchange(send_a, recv_a, 0)

    for load in loads[3:]:
        load.wait()

    cell_of = lax.broadcasted_iota(jnp.int32, (cells, 128), 0)
    cell_of_t = lax.broadcasted_iota(jnp.int32, (128, cells), 1)
    level_of = lax.broadcasted_iota(jnp.int32, (num_levels, 128), 0)
    columns = column_ref[...]
    columns_t = jnp.transpose(columns)
    slot_of = lax.broadcasted_iota(jnp.int32, (slot_rows, 128), 0) * 128 + lax.broadcasted_iota(
        jnp.int32, (slot_rows, 128), 1
    )
    live = (slot_of < count_ref[0]) & (flag_ref[...] > 0)
    for r in range(slot_rows):
        part = slice(r * 128, (r + 1) * 128)
        pick[:, part] = jnp.where(cell_of == columns[r : r + 1, :], 1.0, 0.0).astype(bf16)
        pick_t[part, :] = jnp.where(cell_of_t == columns_t[:, r : r + 1], 1.0, 0.0).astype(bf16)
        at_level[:, part] = jnp.where(level_of == level_ref[r : r + 1, :], 1.0, 0.0).astype(bf16)
        for v in range(num_vars):
            value_rows[v, r : r + 1, :] = value_ref[v : v + 1, part]
            weight_rows[v, r : r + 1, :] = weight_ref[v : v + 1, part]
    for v in range(num_vars):
        vertical_t[v] = jnp.transpose(vertical_ref[v].astype(f32)).astype(bf16)
        weight_rows[v] = jnp.where(live, weight_rows[v], 0.0)

    arrived(recv_a, 0)
    held = [recv_a[i].reshape(num_levels, width).astype(f32) for i in range(rows)]

    step = 256
    for v in range(num_vars):
        product = jnp.concatenate(
            [(perturb_ref[v * rows + i].astype(f32) * held[i]).astype(bf16) for i in range(rows)], axis=1
        )
        increment = dot(vertical_ref[v], product).astype(bf16)
        for t in range(slots // step):
            met = dot(increment, pick[:, t * step : (t + 1) * step])
            for h in range(step // 128):
                r = t * (step // 128) + h
                here = level_of == level_ref[r : r + 1, :]
                block = met[:, h * 128 : (h + 1) * 128]
                at_row[v, r : r + 1, :] = jnp.sum(jnp.where(here, block, 0.0), axis=0, keepdims=True)
        at_mine[v] = at_row[v].astype(bf16)
        pltpu.make_async_copy(at_mine.at[v], at_all.at[v, member], at_recv_sem.at[v]).start()
        for far in NARROW_FAR_FIRST:
            pltpu.make_async_remote_copy(
                src_ref=at_mine.at[v],
                dst_ref=at_all.at[v, member],
                send_sem=at_send_sem.at[v],
                recv_sem=at_recv_sem.at[v],
                device_id={"narrow": lax.rem(member + far, nn)},
                device_id_type=MESH,
            ).start()

    adjoint = []
    for v in range(num_vars):
        pltpu.make_async_copy(at_all.at[v], at_all.at[v], at_recv_sem.at[v]).wait()
        at_obs = at_all[v, 0].astype(f32)
        for k in range(1, nn):
            at_obs = at_obs + at_all[v, k].astype(f32)
        misfit = weight_rows[v] * (at_obs - value_rows[v])
        for r in range(slot_rows):
            part = slice(r * 128, (r + 1) * 128)
            row = jnp.broadcast_to(misfit[r : r + 1, :], (num_levels, 128)).astype(bf16)
            spread[v, :, part] = at_level[:, part] * row
        adjoint.append(dot(spread[v], pick_t[...]).astype(bf16))

    sums = [None] * rows
    for v in range(num_vars):
        lifted = dot(vertical_t[v], adjoint[v]).astype(bf16).astype(f32)
        for i in range(rows):
            term = perturb_ref[v * rows + i].astype(f32) * lifted[:, i * width : (i + 1) * width]
            sums[i] = term if sums[i] is None else sums[i] + term
    for i in range(rows):
        send_b[i] = sums[i].astype(bf16).reshape(send_b.shape[1:])
    exchange(send_b, recv_b, 1)
    arrived(recv_b, 1)

    level_grad = recv_b[...].reshape(rows * blocks * levels, width)
    gradient = own_weights.astype(f32)
    for s, mix in enumerate(scale_mix):
        back = dot(level_grad, table_ref[s]).astype(bf16)
        gradient = gradient + mix * dot(to_levels_ref[s], back)
    out_ref[...] = gradient

    departed(send_a, 0)
    departed(send_b, 1)
    for v in range(num_vars):
        part = at_all.at[v, pl.ds(0, nn - 1)]
        pltpu.make_async_copy(part, part, at_send_sem.at[v]).wait()


def solution(mesh):
    nw, nn = mesh.shape["wide"], mesh.shape["narrow"]

    def local(weights, perturb, vertical, obs_column, obs_level, obs_count, flag, obs_value, obs_weight):
        _, levels, length, width = weights.shape
        _, num_vars, rows, num_levels, _ = perturb.shape
        slots = obs_column.shape[0]
        slot_rows = slots // 128
        tables = [gauss_table(length, spread) for spread in scale_lengths]
        to_rows = np.stack([row_table(table, nw, levels) for table in tables])
        to_levels = np.ascontiguousarray(to_rows.transpose(0, 2, 1))
        operands = (
            weights.reshape(levels * length, width),
            jnp.asarray(to_rows),
            jnp.asarray(np.stack(tables)),
            obs_column.reshape(slot_rows, 128),
            obs_level.reshape(slot_rows, 128),
            vertical,
            perturb.reshape(num_vars * rows, num_levels, width),
            flag.reshape(slot_rows, 128),
            obs_value,
            obs_weight,
            jnp.asarray(to_levels),
        )
        chunk = pltpu.VMEM((rows, nw, levels, width), bf16)
        vmem = pl.BlockSpec(memory_space=pltpu.VMEM)
        out = pl.pallas_call(
            functools.partial(kernel, nw, nn),
            out_shape=pltpu.VMEM((levels * length, width), f32),
            in_specs=[pl.BlockSpec(memory_space=pltpu.SMEM)] + [pl.BlockSpec(memory_space=pltpu.HBM)] * NUM_LOADS,
            out_specs=vmem,
            scratch_shapes=[pltpu.VMEM(operand.shape, operand.dtype) for operand in operands]
            + [
                pltpu.SemaphoreType.DMA((NUM_LOADS,)),
                chunk,
                chunk,
                pltpu.VMEM((num_vars, slot_rows, 128), f32),
                pltpu.VMEM((num_vars, slot_rows, 128), bf16),
                pltpu.VMEM((num_vars, nn, slot_rows, 128), bf16),
                chunk,
                chunk,
                pltpu.VMEM((rows * width, slots), bf16),
                pltpu.VMEM((slots, rows * width), bf16),
                pltpu.VMEM((num_vars, num_levels, slots), bf16),
                pltpu.VMEM((num_vars, num_levels, num_levels), bf16),
                pltpu.VMEM((num_levels, slots), bf16),
                pltpu.VMEM((num_vars, slot_rows, 128), f32),
                pltpu.VMEM((num_vars, slot_rows, 128), f32),
                pltpu.SemaphoreType.DMA((2,)),
                pltpu.SemaphoreType.DMA((2,)),
                pltpu.SemaphoreType.DMA((num_vars,)),
                pltpu.SemaphoreType.DMA((num_vars,)),
            ],
            compiler_params=pltpu.CompilerParams(
                collective_id=0, has_side_effects=True, vmem_limit_bytes=32 * 1024 * 1024
            ),
        )(
            obs_count,
            *(
                pltpu.with_memory_space_constraint(operand, pltpu.HBM)
                for operand in operands
            )
        )
        return out.reshape(weights.shape)

    placed = (
        P("narrow", "wide", None, None),
        P("narrow", None, "wide", None, None),
        P(),
        P("wide"),
        P("wide"),
        P("wide"),
        P("wide"),
        P(None, "wide"),
        P(None, "wide"),
    )
    return jax.shard_map(
        local,
        mesh=mesh,
        in_specs=placed,
        out_specs=P("narrow", "wide", None, None),
        check_vma=False,
    )
```

time: 41 us -> 38.5 us (0.939)
  Pallas kernels: 38.7 us -> 37 us
  local copies, waits for them, and re-layouts: 1.57 us -> 0.66 us
    pallas_call x1, Pallas kernels: 38.7 us -> 37 us  [local(): pl.pallas_call(functools.partial(kernel, nw, nn), out_shape=pltpu.VMEM((l...]
    unnamed x1, local copies, waits for them, and re-layouts: 1.57 us -> 0.66 us
where the time goes in v3:
time: 38.5 us; the launch traced here: 38.3 us
  Pallas kernels  37 us (96%)
  local copies, waits for them, and re-layouts  0.66 us (2%)
  between operations  0.66 us (2%)
    pallas_call x1, Pallas kernels, local(): pl.pallas_call(functools.partial(kernel, nw, nn), out_shape=pltpu.VMEM((l...  37 us

profile of v3, /device:TPU:1, one launch (start us, length us, event | category | flops | bytes accessed | tf_op | source)
XLA Modules:
  0.0 38.3 jit_solution(16033106387865114743)
XLA Ops:
  0.7 37.0 %shard_map.118 = f32[256,128]{1,0:T(8,128)S(1)} custom-call(s32[1]{0:T(128)S(6)} %copy.15.count_ref, bf16[256,128]{1,0:T(8,128)(2,1)} %bitcast.8, bf16[3,256,256]{2,1,0:T(8,128)(2,1)} %constant.6.clone.refs_1_, bf16[3,128,128]{2,1,0:T(8,128)(2,1)} %constant.7.clone.refs_2_, s32[16,128]{1,0:T(8,128)} %bitcast.9, s32[16,128]{1,0:T(8,128)} %bitcast.10, ...), custom_call_target="tpu_custom_call" | custom-call | tf_op jit(solution)/shard_map/pallas_call | solution.py:232
  37.7 0.7 %copy.14 = f32[1,2,128,128]{3,2,1,0:T(8,128)} copy(f32[1,2,128,128]{3,2,1,0:T(8,128)S(1)} %bitcast.6) | data formatting | bytes 262144

commit v4 on v3

--- a/solution.py
+++ b/solution.py
@@ -30,8 +30,8 @@
 def row_table(table, blocks, levels):
     length = table.shape[0]
     rows = length // blocks
-    wide = np.zeros((rows, blocks, levels, levels, length), ml_dtypes.bfloat16)
-    by_row = table.reshape(blocks, rows, length).transpose(1, 0, 2)
+    wide = np.zeros((blocks, rows, levels, levels, length), ml_dtypes.bfloat16)
+    by_row = table.reshape(blocks, rows, length)
     for level in range(levels):
         wide[:, :, level, level, :] = by_row
     return wide.reshape(rows * blocks * levels, levels * length)
@@ -53,12 +53,12 @@
     ) = loaded
     (
         load_sem, send_a, recv_a, at_row, at_mine, at_all, send_b, recv_b, pick, pick_t, spread, vertical_t,
-        at_level, value_rows, weight_rows,
+        at_level, lift, lift_low, value_rows, weight_rows,
     send_sem, recv_sem, at_send_sem, at_recv_sem,
     ) = refs[2 * NUM_LOADS + 1 :]
     me = lax.axis_index("wide")
     member = lax.axis_index("narrow")
-    rows, blocks, levels, width = send_a.shape
+    blocks, rows, levels, width = send_a.shape
     num_vars, num_levels, _ = vertical_ref.shape
     slot_rows = column_ref.shape[0]
     slots = slot_rows * 128
@@ -79,14 +79,14 @@
         load.start()
 
     def exchange(source, target, phase):
-        own = pltpu.make_async_copy(source.at[:, me], target.at[:, me], recv_sem.at[phase])
+        own = pltpu.make_async_copy(source.at[me], target.at[me], recv_sem.at[phase])
         own.start()
 
         for far in FAR_FIRST:
             peer = lax.rem(me + far, nw)
             pltpu.make_async_remote_copy(
-                src_ref=source.at[:, peer],
-                dst_ref=target.at[:, me],
+                src_ref=source.at[peer],
+                dst_ref=target.at[me],
                 send_sem=send_sem.at[phase],
                 recv_sem=recv_sem.at[phase],
                 device_id={"wide": peer},
@@ -97,7 +97,7 @@
         pltpu.make_async_copy(target, target, recv_sem.at[phase]).wait()
 
     def departed(source, phase):
-        part = source.at[:, pl.ds(0, nw - 1)]
+        part = source.at[pl.ds(0, nw - 1)]
         pltpu.make_async_copy(part, part, send_sem.at[phase]).wait()
 
     for load in loads[:3]:
@@ -136,23 +136,27 @@
     for v in range(num_vars):
         vertical_t[v] = jnp.transpose(vertical_ref[v].astype(f32)).astype(bf16)
         weight_rows[v] = jnp.where(live, weight_rows[v], 0.0)
+    step = 256
+    for v in range(num_vars):
+        for t in range(slots // step):
+            part = slice(t * step, (t + 1) * step)
+            rows_of = dot(vertical_t[v], at_level[:, part])
+            lift[v, :, part] = rows_of
+            lift_low[v, :, part] = rows_of.astype(bf16)
 
     arrived(recv_a, 0)
-    held = [recv_a[i].reshape(num_levels, width).astype(f32) for i in range(rows)]
-
-    step = 256
+    held = [recv_a[:, i].reshape(num_levels, width).astype(f32) for i in range(rows)]
+
     for v in range(num_vars):
         product = jnp.concatenate(
             [(perturb_ref[v * rows + i].astype(f32) * held[i]).astype(bf16) for i in range(rows)], axis=1
         )
-        increment = dot(vertical_ref[v], product).astype(bf16)
         for t in range(slots // step):
-            met = dot(increment, pick[:, t * step : (t + 1) * step])
+            met = dot(product, pick[:, t * step : (t + 1) * step])
             for h in range(step // 128):
                 r = t * (step // 128) + h
-                here = level_of == level_ref[r : r + 1, :]
-                block = met[:, h * 128 : (h + 1) * 128]
-                at_row[v, r : r + 1, :] = jnp.sum(jnp.where(here, block, 0.0), axis=0, keepdims=True)
+                block = met[:, h * 128 : (h + 1) * 128] * lift[v, :, r * 128 : (r + 1) * 128]
+                at_row[v, r : r + 1, :] = jnp.sum(block, axis=0, keepdims=True)
         at_mine[v] = at_row[v].astype(bf16)
         pltpu.make_async_copy(at_mine.at[v], at_all.at[v, member], at_recv_sem.at[v]).start()
         for far in NARROW_FAR_FIRST:
@@ -165,7 +169,7 @@
                 device_id_type=MESH,
             ).start()
 
-    adjoint = []
+    sums = [None] * rows
     for v in range(num_vars):
         pltpu.make_async_copy(at_all.at[v], at_all.at[v], at_recv_sem.at[v]).wait()
         at_obs = at_all[v, 0].astype(f32)
@@ -175,25 +179,19 @@
         for r in range(slot_rows):
             part = slice(r * 128, (r + 1) * 128)
             row = jnp.broadcast_to(misfit[r : r + 1, :], (num_levels, 128)).astype(bf16)
-            spread[v, :, part] = at_level[:, part] * row
-        adjoint.append(dot(spread[v], pick_t[...]).astype(bf16))
-
-    sums = [None] * rows
-    for v in range(num_vars):
-        lifted = dot(vertical_t[v], adjoint[v]).astype(bf16).astype(f32)
+            spread[v, :, part] = lift_low[v, :, part] * row
+        lifted = dot(spread[v], pick_t[...]).astype(bf16).astype(f32)
         for i in range(rows):
             term = perturb_ref[v * rows + i].astype(f32) * lifted[:, i * width : (i + 1) * width]
             sums[i] = term if sums[i] is None else sums[i] + term
     for i in range(rows):
-        send_b[i] = sums[i].astype(bf16).reshape(send_b.shape[1:])
+        send_b[:, i] = sums[i].astype(bf16).reshape(blocks, levels, width)
     exchange(send_b, recv_b, 1)
     arrived(recv_b, 1)
 
     level_grad = recv_b[...].reshape(rows * blocks * levels, width)
-    gradient = own_weights.astype(f32)
-    for s, mix in enumerate(scale_mix):
-        back = dot(level_grad, table_ref[s]).astype(bf16)
-        gradient = gradient + mix * dot(to_levels_ref[s], back)
+    back = [(mix * dot(level_grad, table_ref[s])).astype(bf16) for s, mix in enumerate(scale_mix)]
+    gradient = own_weights.astype(f32) + dot(to_levels_ref[...], jnp.concatenate(back, axis=0))
     out_ref[...] = gradient
 
     departed(send_a, 0)
@@ -213,7 +211,7 @@
         slot_rows = slots // 128
         tables = [gauss_table(length, spread) for spread in scale_lengths]
         to_rows = np.stack([row_table(table, nw, levels) for table in tables])
-        to_levels = np.ascontiguousarray(to_rows.transpose(0, 2, 1))
+        to_levels = np.concatenate(list(to_rows.transpose(0, 2, 1)), axis=1)
         operands = (
             weights.reshape(levels * length, width),
             jnp.asarray(to_rows),
@@ -227,7 +225,7 @@
             obs_weight,
             jnp.asarray(to_levels),
         )
-        chunk = pltpu.VMEM((rows, nw, levels, width), bf16)
+        chunk = pltpu.VMEM((nw, rows, levels, width), bf16)
         vmem = pl.BlockSpec(memory_space=pltpu.VMEM)
         out = pl.pallas_call(
             functools.partial(kernel, nw, nn),
@@ -249,6 +247,8 @@
                 pltpu.VMEM((num_vars, num_levels, slots), bf16),
                 pltpu.VMEM((num_vars, num_levels, num_levels), bf16),
                 pltpu.VMEM((num_levels, slots), bf16),
+                pltpu.VMEM((num_vars, num_levels, slots), f32),
+                pltpu.VMEM((num_vars, num_levels, slots), bf16),
                 pltpu.VMEM((num_vars, slot_rows, 128), f32),
                 pltpu.VMEM((num_vars, slot_rows, 128), f32),
                 pltpu.SemaphoreType.DMA((2,)),

time: 38.5 us -> 38.2 us (level)
  no operation moved by 1% of the time
where the time goes in v4:
time: 38.2 us; the launch traced here: 38.1 us
  Pallas kernels  36.7 us (96%)
  local copies, waits for them, and re-layouts  0.66 us (2%)
  between operations  0.66 us (2%)
    pallas_call x1, Pallas kernels, local(): pl.pallas_call(functools.partial(kernel, nw, nn), out_shape=pltpu.VMEM((l...  36.7 us

profile of v4, /device:TPU:1, one launch (start us, length us, event | category | flops | bytes accessed | tf_op | source)
XLA Modules:
  0.0 38.1 jit_solution(6486061100090815345)
XLA Ops:
  0.7 36.7 %shard_map.118 = f32[256,128]{1,0:T(8,128)S(1)} custom-call(s32[1]{0:T(128)S(6)} %copy.15.count_ref, bf16[256,128]{1,0:T(8,128)(2,1)} %bitcast.8, bf16[3,256,256]{2,1,0:T(8,128)(2,1)} %constant.6.clone.refs_1_, bf16[3,128,128]{2,1,0:T(8,128)(2,1)} %constant.7.clone.refs_2_, s32[16,128]{1,0:T(8,128)} %bitcast.9, s32[16,128]{1,0:T(8,128)} %bitcast.10, ...), custom_call_target="tpu_custom_call" | custom-call | tf_op jit(solution)/shard_map/pallas_call | solution.py:230
  37.4 0.7 %copy.14 = f32[1,2,128,128]{3,2,1,0:T(8,128)} copy(f32[1,2,128,128]{3,2,1,0:T(8,128)S(1)} %bitcast.6) | data formatting | bytes 262144

commit v5 on v4

--- a/solution.py
+++ b/solution.py
@@ -35,6 +35,10 @@
     for level in range(levels):
         wide[:, :, level, level, :] = by_row
     return wide.reshape(rows * blocks * levels, levels * length)
+
+
+def wrap(index, count):
+    return jnp.where(index >= count, index - count, index)
 
 
 def dot(a, b):
@@ -67,7 +71,7 @@
     barrier = pltpu.get_barrier_semaphore()
 
     for far in FAR_FIRST:
-        peer = lax.rem(me + far, nw)
+        peer = wrap(me + far, nw)
         pl.semaphore_signal(barrier, inc=1, device_id={"wide": peer}, device_id_type=MESH)
     for k in range(1, nn):
         pl.semaphore_signal(
@@ -79,11 +83,8 @@
         load.start()
 
     def exchange(source, target, phase):
-        own = pltpu.make_async_copy(source.at[me], target.at[me], recv_sem.at[phase])
-        own.start()
-
         for far in FAR_FIRST:
-            peer = lax.rem(me + far, nw)
+            peer = wrap(me + far, nw)
             pltpu.make_async_remote_copy(
                 src_ref=source.at[peer],
                 dst_ref=target.at[me],
@@ -92,6 +93,7 @@
                 device_id={"wide": peer},
                 device_id_type=MESH,
             ).start()
+        pltpu.make_async_copy(source.at[me], target.at[me], recv_sem.at[phase]).start()
 
     def arrived(target, phase):
         pltpu.make_async_copy(target, target, recv_sem.at[phase]).wait()
@@ -151,14 +153,14 @@
         product = jnp.concatenate(
             [(perturb_ref[v * rows + i].astype(f32) * held[i]).astype(bf16) for i in range(rows)], axis=1
         )
+        met_rows = []
         for t in range(slots // step):
             met = dot(product, pick[:, t * step : (t + 1) * step])
             for h in range(step // 128):
                 r = t * (step // 128) + h
                 block = met[:, h * 128 : (h + 1) * 128] * lift[v, :, r * 128 : (r + 1) * 128]
-                at_row[v, r : r + 1, :] = jnp.sum(block, axis=0, keepdims=True)
-        at_mine[v] = at_row[v].astype(bf16)
-        pltpu.make_async_copy(at_mine.at[v], at_all.at[v, member], at_recv_sem.at[v]).start()
+                met_rows.append(jnp.sum(block, axis=0, keepdims=True))
+        at_mine[v] = jnp.concatenate(met_rows, axis=0).astype(bf16)
         for far in NARROW_FAR_FIRST:
             pltpu.make_async_remote_copy(
                 src_ref=at_mine.at[v],
@@ -168,6 +170,7 @@
                 device_id={"narrow": lax.rem(member + far, nn)},
                 device_id_type=MESH,
             ).start()
+        pltpu.make_async_copy(at_mine.at[v], at_all.at[v, member], at_recv_sem.at[v]).start()
 
     sums = [None] * rows
     for v in range(num_vars):

time: 38.2 us -> 38.3 us (level)
  no operation moved by 1% of the time
where the time goes in v5:
time: 38.3 us; the launch traced here: 38.1 us
  Pallas kernels  36.8 us (96%)
  local copies, waits for them, and re-layouts  0.66 us (2%)
  between operations  0.66 us (2%)
    pallas_call x1, Pallas kernels, local(): pl.pallas_call(functools.partial(kernel, nw, nn), out_shape=pltpu.VMEM((l...  36.8 us

profile of v5, /device:TPU:1, one launch (start us, length us, event | category | flops | bytes accessed | tf_op | source)
XLA Modules:
  0.0 38.1 jit_solution(15863449223002942249)
XLA Ops:
  0.7 36.8 %shard_map.118 = f32[256,128]{1,0:T(8,128)S(1)} custom-call(s32[1]{0:T(128)S(6)} %copy.15.count_ref, bf16[256,128]{1,0:T(8,128)(2,1)} %bitcast.8, bf16[3,256,256]{2,1,0:T(8,128)(2,1)} %constant.6.clone.refs_1_, bf16[3,128,128]{2,1,0:T(8,128)(2,1)} %constant.7.clone.refs_2_, s32[16,128]{1,0:T(8,128)} %bitcast.9, s32[16,128]{1,0:T(8,128)} %bitcast.10, ...), custom_call_target="tpu_custom_call" | custom-call | tf_op jit(solution)/shard_map/pallas_call | solution.py:233
  37.5 0.7 %copy.14 = f32[1,2,128,128]{3,2,1,0:T(8,128)} copy(f32[1,2,128,128]{3,2,1,0:T(8,128)S(1)} %bitcast.6) | data formatting | bytes 262144
